TPU v7x, 256 devices: a whole 4x4x8 slice. The times are simulated.
256 devices in a mesh: leaf: 256 (over z, x, y, core).
Axes of the slice: x: 4, y: 4, z: 8, core: 2. Of those that a mesh axis runs over, the one named last changes fastest.
Arguments:
- sources: float32 [2, 4096, 8, 256], P(None, 'leaf'), may hold values from -6 to 6
- leaf_slot: int32 [4096], replicated, may hold values from 0 to 4095, as said below
- in_basis: float32 [4096, 2, 64, 256], P('leaf'), may hold values from -0.25 to 0.25
- butterfly: float32 [8, 256, 2, 64, 128], P(None, 'leaf'), may hold values from -0.375 to 0.375
- out_basis: float32 [4096, 2, 64, 256], P('leaf'), may hold values from -0.5 to 0.5
- near_pairs: int32 [2048, 2], P('leaf'), may hold values from 0 to 4095, as said below
- near_count: int32 [256], P('leaf'), may hold values from 1 to 8, as said below
- near_blocks: float32 [2048, 2, 256, 256], P('leaf'), may hold values from -0.25 to 0.25
Outputs:
- field: float32 [2, 4096, 8, 256], P(None, 'leaf')
Inputs may be any that keep to these rules, and one draw needn't show every extreme that they name: Leaf l is stored on its own device: leaf_slot restricted to leaves d * 16 .. (d + 1) * 16 - 1 is a permutation of those same slots. `near_pairs`: column 0 is the source leaf, column 1 the target leaf. The target leaf of a slot of device d is one of d's leaves d * 16 .. (d + 1) * 16 - 1, and source and target leaves lie at most 4 apart along the line. `near_count`: some device has all 8 slots live.
All inputs are finite; a program needn't handle non-finite values.
Results may differ from a plain program's by a relative error of at most 0.00011.
Values sent between devices are 32-bit elements; how exact they have to be, the bound alone decides.
A program may use at most 64 MiB of HBM per device.

v0:
```python
import jax
import jax.numpy as jnp
from jax import lax
from jax.sharding import PartitionSpec as P

HIGH = lax.Precision.HIGHEST


def from_partner(x, axis, bit):
    return lax.ppermute(x, axis, [(i, i ^ 1 << bit) for i in range(lax.axis_size(axis))])


def padded_2(x, sides, width):
    for axis, dim in sides:
        size, length = (lax.axis_size(axis), x.shape[dim])
        up = [(i, (i + 1) % size) for i in range(size - 1)]
        down = [(j, i) for i, j in up]
        last = lax.slice_in_dim(x, length - width, length, axis=dim)
        leading = lax.slice_in_dim(x, 0, width, axis=dim)
        before = lax.ppermute(last, axis, up)
        after = lax.ppermute(leading, axis, down)
        x = jnp.concatenate([before, x, after], axis=dim)
    return x


def apply_block(blocks, panel):
    rank = blocks.shape[0]
    w_real = blocks[:, :rank]
    w_imag = blocks[:, rank:]
    real_part = jnp.dot(
        w_real, panel[0], precision=HIGH, preferred_element_type=jnp.float32
    ) - jnp.dot(w_imag, panel[1], precision=HIGH, preferred_element_type=jnp.float32)
    imag_part = jnp.dot(
        w_real, panel[1], precision=HIGH, preferred_element_type=jnp.float32
    ) + jnp.dot(w_imag, panel[0], precision=HIGH, preferred_element_type=jnp.float32)
    return jnp.stack([real_part, imag_part])


def body(sources, leaf_slot, in_basis, butterfly, out_basis, near_pairs, near_count, near_blocks):
    leaf_count = sources.shape[1]
    source_count = sources.shape[2]
    rank = in_basis.shape[2]
    levels_total = butterfly.shape[0]
    coeff_real = jnp.einsum(
        "lrp,lsp->rls", in_basis[:, 0], sources[0], precision=HIGH
    ) - jnp.einsum("lrp,lsp->rls", in_basis[:, 1], sources[1], precision=HIGH)
    coeff_imag = jnp.einsum(
        "lrp,lsp->rls", in_basis[:, 0], sources[1], precision=HIGH
    ) + jnp.einsum("lrp,lsp->rls", in_basis[:, 1], sources[0], precision=HIGH)
    panel = jnp.stack([coeff_real, coeff_imag]).reshape(2, rank, leaf_count * source_count)
    for level_bit in range(levels_total):
        other = from_partner(panel, "leaf", level_bit)
        panel = apply_block(butterfly[level_bit, 0, 0], panel) + apply_block(
            butterfly[level_bit, 0, 1], other
        )
    final = panel.reshape(2, rank, leaf_count, source_count)
    far_real = jnp.einsum("rls,lrp->lsp", final[0], out_basis[:, 0], precision=HIGH) - jnp.einsum(
        "rls,lrp->lsp", final[1], out_basis[:, 1], precision=HIGH
    )
    far_imag = jnp.einsum("rls,lrp->lsp", final[1], out_basis[:, 0], precision=HIGH) + jnp.einsum(
        "rls,lrp->lsp", final[0], out_basis[:, 1], precision=HIGH
    )
    base = lax.axis_index("leaf") * leaf_count
    padded = padded_2(sources, (("leaf", 1),), leaf_count)
    src_local = jnp.take(leaf_slot, near_pairs[:, 0]) - base + leaf_count
    picked = jnp.take(padded, src_local, axis=1)
    term_real = jnp.einsum(
        "bpq,bsq->bsp", near_blocks[:, 0], picked[0], precision=HIGH
    ) - jnp.einsum("bpq,bsq->bsp", near_blocks[:, 1], picked[1], precision=HIGH)
    term_imag = jnp.einsum(
        "bpq,bsq->bsp", near_blocks[:, 0], picked[1], precision=HIGH
    ) + jnp.einsum("bpq,bsq->bsp", near_blocks[:, 1], picked[0], precision=HIGH)
    slot_count = near_pairs.shape[0]
    live = (jnp.arange(slot_count, dtype=jnp.int32) < near_count[0]).astype(jnp.float32)
    tgt_local = jnp.take(leaf_slot, near_pairs[:, 1]) - base
    placing = (jnp.arange(leaf_count, dtype=jnp.int32)[:, None] == tgt_local[None, :]).astype(
        jnp.float32
    ) * live[None, :]
    near_real = jnp.einsum("lb,bsp->lsp", placing, term_real, precision=HIGH)
    near_imag = jnp.einsum("lb,bsp->lsp", placing, term_imag, precision=HIGH)
    return jnp.stack([far_real + near_real, far_imag + near_imag])


def solution(mesh):
    in_specs = (
        P(None, "leaf", None, None),
        P(),
        P("leaf", None, None, None),
        P(None, "leaf", None, None, None),
        P("leaf", None, None, None),
        P("leaf", None),
        P("leaf"),
        P("leaf", None, None, None),
    )
    out_specs = P(None, "leaf", None, None)
    return jax.shard_map(body, mesh=mesh, in_specs=in_specs, out_specs=out_specs, check_vma=False)
```

profile of v0, /device:TPU:26, one launch (start us, length us, event | category | flops | bytes accessed | tf_op | source)
XLA Modules:
  0.0 83.6 jit_solution(3517015222803902612)
XLA Ops:
  0.0 2.2 %collective-permute-start.9 = (f32[2,16,8,256]{3,2,1,0:T(8,128)}, f32[2,16,8,256]{3,2,1,0:T(8,128)S(1)}, u32[]{:S(2)}, u32[]{:S(2)}) collective-permute-start(f32[2,16,8,256]{3,2,1,0:T(8,128)} %param.10), channel_id=1, source_target_pairs={{1,0},{2,1},{3,2},{4,3},{5,4},{6,5},{7,6},{8,7},{9,8},{10,9},{11,1... | collective-permute-start | bytes 786440 | tf_op jit(solution)/shard_map/ppermute | solution.py:21
  2.2 2.2 %collective-permute-start.8 = (f32[2,16,8,256]{3,2,1,0:T(8,128)}, f32[2,16,8,256]{3,2,1,0:T(8,128)S(1)}, u32[]{:S(2)}, u32[]{:S(2)}) collective-permute-start(f32[2,16,8,256]{3,2,1,0:T(8,128)} %param.10), channel_id=1, source_target_pairs={{0,1},{1,2},{2,3},{3,4},{4,5},{5,6},{6,7},{7,8},{8,9},{9,10},{10,1... | collective-permute-start | bytes 786440 | tf_op jit(solution)/shard_map/ppermute | solution.py:20
  4.5 2.3 %fusion.56 = f32[16,8,64]{2,1,0:T(8,128)S(1)} fusion(f32[16,2,64,256]{3,2,1,0:T(8,128)} %param.12, f32[2,16,8,256]{3,2,1,0:T(8,128)} %param.10), kind=kOutput, calls=%fused_computation.95 | convolution fusion | flops 25165824 | bytes 1212416 | tf_op jit(solution)/shard_map/lrp,lsp->rls/dot_general | solution.py:47
  6.8 2.3 %fusion.58 = f32[16,8,64]{2,1,0:T(8,128)S(1)} fusion(f32[16,2,64,256]{3,2,1,0:T(8,128)} %param.12, f32[2,16,8,256]{3,2,1,0:T(8,128)} %param.10), kind=kOutput, calls=%fused_computation.97 | convolution fusion | flops 25165824 | bytes 1212416 | tf_op jit(solution)/shard_map/lrp,lsp->rls/dot_general | solution.py:44
  9.1 1.0 %convolution_add_fusion.1 = f32[16,8,64]{2,1,0:T(8,128)S(1)} fusion(f32[16,8,64]{2,1,0:T(8,128)S(1)} %fusion.56, f32[16,2,64,256]{3,2,1,0:T(8,128)S(1)} %copy-done.2, f32[2,16,8,256]{3,2,1,0:T(8,128)S(1)} %copy-done.4), kind=kOutput, calls=%fused_computation.21 | convolution fusion | flops 25174016 | bytes 1277952 | tf_op jit(solution)/shard_map/lrp,lsp->rls/dot_general | solution.py:49
  10.0 1.0 %convolution_subtract_fusion.1 = f32[16,8,64]{2,1,0:T(8,128)S(1)} fusion(f32[16,8,64]{2,1,0:T(8,128)S(1)} %fusion.58, f32[16,2,64,256]{3,2,1,0:T(8,128)S(1)} %copy-done.2, f32[2,16,8,256]{3,2,1,0:T(8,128)S(1)} %copy-done.4), kind=kOutput, calls=%fused_computation.22 | convolution fusion | flops 25174016 | bytes 1277952 | tf_op jit(solution)/shard_map/lrp,lsp->rls/dot_general | solution.py:46
  11.0 3.3 %collective-permute-start = (f32[2,64,128]{1,2,0:T(8,128)S(1)}, f32[2,64,128]{1,2,0:T(8,128)S(1)}, u32[]{:S(2)}, u32[]{:S(2)}) collective-permute-start(f32[2,64,128]{1,2,0:T(8,128)S(1)} %pad_maximum_fusion.2), channel_id=1, source_target_pairs={{0,1},{1,0},{2,3},{3,2},{4,5},{5,4},{6,7},{7,6},{8,9},{9,8},{10,11... | collective-permute-start | bytes 196616 | tf_op jit(solution)/shard_map/ppermute | solution.py:10
  15.5 0.6 gather_fusion.1
  16.2 0.6 gather_fusion.2
  19.5 3.8 %collective-permute-done.1 = f32[2,64,128]{2,1,0:T(8,128)S(1)} collective-permute-done((f32[2,64,128]{2,1,0:T(8,128)S(1)}, f32[2,64,128]{2,1,0:T(8,128)S(1)}, u32[]{:S(2)}, u32[]{:S(2)}) %collective-permute-start.1) | collective-permute-done | bytes 65568 | tf_op jit(solution)/shard_map/ppermute | solution.py:10
  25.0 5.3 %collective-permute-done.2 = f32[2,64,128]{2,1,0:T(8,128)S(1)} collective-permute-done((f32[2,64,128]{2,1,0:T(8,128)S(1)}, f32[2,64,128]{2,1,0:T(8,128)S(1)}, u32[]{:S(2)}, u32[]{:S(2)}) %collective-permute-start.2) | collective-permute-done | bytes 65568 | tf_op jit(solution)/shard_map/ppermute | solution.py:10
  32.6 3.3 %collective-permute-done.3 = f32[2,64,128]{2,1,0:T(8,128)S(1)} collective-permute-done((f32[2,64,128]{2,1,0:T(8,128)S(1)}, f32[2,64,128]{2,1,0:T(8,128)S(1)}, u32[]{:S(2)}, u32[]{:S(2)}) %collective-permute-start.3) | collective-permute-done | bytes 65568 | tf_op jit(solution)/shard_map/ppermute | solution.py:10
  36.6 4.7 %collective-permute-start.4 = (f32[2,64,128]{2,1,0:T(8,128)S(1)}, f32[2,64,128]{2,1,0:T(8,128)S(1)}, u32[]{:S(2)}, u32[]{:S(2)}) collective-permute-start(f32[2,64,128]{2,1,0:T(8,128)S(1)} %maximum_add_fusion.3), channel_id=1, source_target_pairs={{0,16},{1,17},{2,18},{3,19},{4,20},{5,21},{6,22},{7,23},{8,24},{9,... | collective-permute-start | bytes 196616 | tf_op jit(solution)/shard_map/ppermute | solution.py:10
  42.4 3.5 %fusion = f32[8,8,256]{2,1,0:T(8,128)S(1)} fusion(f32[8,2,256,256]{3,2,1,0:T(8,128)} %param.17, f32[2,8,8,256]{3,2,0,1:T(8,128)S(1)} %select_bitcast_fusion), kind=kOutput, calls=%fused_computation.3 | convolution fusion | flops 50331648 | bytes 2228224 | tf_op jit(solution)/shard_map/bpq,bsq->bsp/dot_general | solution.py:72
  46.0 3.4 %fusion.4 = f32[8,8,256]{2,1,0:T(8,128)S(1)} fusion(f32[8,2,256,256]{3,2,1,0:T(8,128)} %param.17, f32[2,8,8,256]{3,2,0,1:T(8,128)S(1)} %select_bitcast_fusion), kind=kOutput, calls=%fused_computation.7 | convolution fusion | flops 50331648 | bytes 2228224 | tf_op jit(solution)/shard_map/bpq,bsq->bsp/dot_general | solution.py:70
  49.4 1.8 %fusion.2 = f32[8,8,256]{2,1,0:T(8,128)S(1)} fusion(f32[8,2,256,256]{3,2,1,0:T(8,128)S(1)} %copy-done.1, f32[2,8,8,256]{3,2,0,1:T(8,128)S(1)} %select_bitcast_fusion), kind=kOutput, calls=%fused_computation.5 | convolution fusion | flops 50331648 | bytes 2228224 | tf_op jit(solution)/shard_map/bpq,bsq->bsp/dot_general | solution.py:69
  51.2 1.8 %fusion.6 = f32[8,8,256]{2,1,0:T(8,128)S(1)} fusion(f32[8,2,256,256]{3,2,1,0:T(8,128)S(1)} %copy-done.1, f32[2,8,8,256]{3,2,0,1:T(8,128)S(1)} %select_bitcast_fusion), kind=kOutput, calls=%fused_computation.9 | convolution fusion | flops 50331648 | bytes 2228224 | tf_op jit(solution)/shard_map/bpq,bsq->bsp/dot_general | solution.py:67
  55.5 2.0 %collective-permute-start.5 = (f32[2,64,128]{2,1,0:T(8,128)S(1)}, f32[2,64,128]{2,1,0:T(8,128)S(1)}, u32[]{:S(2)}, u32[]{:S(2)}) collective-permute-start(f32[2,64,128]{2,1,0:T(8,128)S(1)} %maximum_add_fusion.4), channel_id=1, source_target_pairs={{0,32},{1,33},{2,34},{3,35},{4,36},{5,37},{6,38},{7,39},{8,40},{9,... | collective-permute-start | bytes 196616 | tf_op jit(solution)/shard_map/ppermute | solution.py:10
  58.0 1.9 %collective-permute-done.5 = f32[2,64,128]{2,1,0:T(8,128)S(1)} collective-permute-done((f32[2,64,128]{2,1,0:T(8,128)S(1)}, f32[2,64,128]{2,1,0:T(8,128)S(1)}, u32[]{:S(2)}, u32[]{:S(2)}) %collective-permute-start.5) | collective-permute-done | bytes 65568 | tf_op jit(solution)/shard_map/ppermute | solution.py:10
  61.0 4.9 %collective-permute-start.6 = (f32[2,64,128]{2,1,0:T(8,128)S(1)}, f32[2,64,128]{2,1,0:T(8,128)S(1)}, u32[]{:S(2)}, u32[]{:S(2)}) collective-permute-start(f32[2,64,128]{2,1,0:T(8,128)S(1)} %maximum_add_fusion.5), channel_id=1, source_target_pairs={{0,64},{1,65},{2,66},{3,67},{4,68},{5,69},{6,70},{7,71},{8,72},{9,... | collective-permute-start | bytes 196616 | tf_op jit(solution)/shard_map/ppermute | solution.py:10
  66.4 1.8 %collective-permute-done.6 = f32[2,64,128]{2,1,0:T(8,128)S(1)} collective-permute-done((f32[2,64,128]{2,1,0:T(8,128)S(1)}, f32[2,64,128]{2,1,0:T(8,128)S(1)}, u32[]{:S(2)}, u32[]{:S(2)}) %collective-permute-start.6) | collective-permute-done | bytes 65568 | tf_op jit(solution)/shard_map/ppermute | solution.py:10
  69.4 7.7 %collective-permute-start.7 = (f32[2,64,128]{2,1,0:T(8,128)S(1)}, f32[2,64,128]{2,1,0:T(8,128)S(1)}, u32[]{:S(2)}, u32[]{:S(2)}) collective-permute-start(f32[2,64,128]{2,1,0:T(8,128)S(1)} %maximum_add_fusion.6), channel_id=1, source_target_pairs={{0,128},{1,129},{2,130},{3,131},{4,132},{5,133},{6,134},{7,135},{8... | collective-permute-start | bytes 196616 | tf_op jit(solution)/shard_map/ppermute | solution.py:10
  77.5 1.8 %collective-permute-done.7 = f32[2,64,128]{2,1,0:T(8,128)S(1)} collective-permute-done((f32[2,64,128]{2,1,0:T(8,128)S(1)}, f32[2,64,128]{2,1,0:T(8,128)S(1)}, u32[]{:S(2)}, u32[]{:S(2)}) %collective-permute-start.7) | collective-permute-done | bytes 65568 | tf_op jit(solution)/shard_map/ppermute | solution.py:10
  82.8 0.7 pad_maximum_fusion.1
  (114 shorter events, 18.1 us)
Async XLA Ops:
  0.0 15.5 %copy-start = (s32[4096]{0:T(1024)S(1)}, s32[4096]{0:T(1024)}, u32[]{:S(2)}) copy-start(s32[4096]{0:T(1024)} %param.11) | copy-start | bytes 49156
  0.0 9.1 %copy-start.4 = (f32[2,16,8,256]{3,2,1,0:T(8,128)S(1)}, f32[2,16,8,256]{3,2,1,0:T(8,128)}, u32[]{:S(2)}) copy-start(f32[2,16,8,256]{3,2,1,0:T(8,128)} %param.10) | copy-start | bytes 786436
  0.0 9.1 %copy-start.2 = (f32[16,2,64,256]{3,2,1,0:T(8,128)S(1)}, f32[16,2,64,256]{3,2,1,0:T(8,128)}, u32[]{:S(2)}) copy-start(f32[16,2,64,256]{3,2,1,0:T(8,128)} %param.12) | copy-start | bytes 6291460
  0.0 41.7 %collective-permute-start.9 = (f32[2,16,8,256]{3,2,1,0:T(8,128)}, f32[2,16,8,256]{3,2,1,0:T(8,128)S(1)}, u32[]{:S(2)}, u32[]{:S(2)}) collective-permute-start(f32[2,16,8,256]{3,2,1,0:T(8,128)} %param.10), channel_id=1, source_target_pairs={{1,0},{2,1},{3,2},{4,3},{5,4},{6,5},{7,6},{8,7},{9,8},{10,9},{11,1... | collective-permute-start | bytes 786440 | tf_op jit(solution)/shard_map/ppermute | solution.py:21
  2.2 39.5 %collective-permute-start.8 = (f32[2,16,8,256]{3,2,1,0:T(8,128)}, f32[2,16,8,256]{3,2,1,0:T(8,128)S(1)}, u32[]{:S(2)}, u32[]{:S(2)}) collective-permute-start(f32[2,16,8,256]{3,2,1,0:T(8,128)} %param.10), channel_id=1, source_target_pairs={{0,1},{1,2},{2,3},{3,4},{4,5},{5,6},{6,7},{7,8},{8,9},{9,10},{10,1... | collective-permute-start | bytes 786440 | tf_op jit(solution)/shard_map/ppermute | solution.py:20
  6.7 7.6 %copy-start.5 = (f32[8,1,2,64,128]{4,3,2,1,0:T(8,128)S(1)}, f32[8,1,2,64,128]{4,3,2,1,0:T(8,128)}, u32[]{:S(2)}) copy-start(f32[8,1,2,64,128]{4,3,2,1,0:T(8,128)} %param.13) | copy-start | bytes 1572868
  9.1 6.4 %copy-start.6 = (s32[8,2]{0,1:T(2,128)S(1)}, s32[8,2]{0,1:T(2,128)}, u32[]{:S(2)}) copy-start(s32[8,2]{0,1:T(2,128)} %param.15) | copy-start | bytes 196
  11.0 6.4 %collective-permute-start = (f32[2,64,128]{1,2,0:T(8,128)S(1)}, f32[2,64,128]{1,2,0:T(8,128)S(1)}, u32[]{:S(2)}, u32[]{:S(2)}) collective-permute-start(f32[2,64,128]{1,2,0:T(8,128)S(1)} %pad_maximum_fusion.2), channel_id=1, source_target_pairs={{0,1},{1,0},{2,3},{3,2},{4,5},{5,4},{6,7},{7,6},{8,9},{9,8},{10,11... | collective-permute-start | bytes 196616 | tf_op jit(solution)/shard_map/ppermute | solution.py:10
  18.9 4.4 %collective-permute-start.1 = (f32[2,64,128]{2,1,0:T(8,128)S(1)}, f32[2,64,128]{2,1,0:T(8,128)S(1)}, u32[]{:S(2)}, u32[]{:S(2)}) collective-permute-start(f32[2,64,128]{2,1,0:T(8,128)S(1)} %maximum_add_fusion), channel_id=1, source_target_pairs={{0,2},{1,3},{2,0},{3,1},{4,6},{5,7},{6,4},{7,5},{8,10},{9,11},{10,... | collective-permute-start | bytes 196616 | tf_op jit(solution)/shard_map/ppermute | solution.py:10
  24.4 5.9 %collective-permute-start.2 = (f32[2,64,128]{2,1,0:T(8,128)S(1)}, f32[2,64,128]{2,1,0:T(8,128)S(1)}, u32[]{:S(2)}, u32[]{:S(2)}) collective-permute-start(f32[2,64,128]{2,1,0:T(8,128)S(1)} %maximum_add_fusion.1), channel_id=1, source_target_pairs={{0,4},{1,5},{2,6},{3,7},{4,0},{5,1},{6,2},{7,3},{8,12},{9,13},{10,... | collective-permute-start | bytes 196616 | tf_op jit(solution)/shard_map/ppermute | solution.py:10
  31.5 4.4 %collective-permute-start.3 = (f32[2,64,128]{2,1,0:T(8,128)S(1)}, f32[2,64,128]{2,1,0:T(8,128)S(1)}, u32[]{:S(2)}, u32[]{:S(2)}) collective-permute-start(f32[2,64,128]{2,1,0:T(8,128)S(1)} %maximum_add_fusion.2), channel_id=1, source_target_pairs={{0,8},{1,9},{2,10},{3,11},{4,12},{5,13},{6,14},{7,15},{8,0},{9,1},... | collective-permute-start | bytes 196616 | tf_op jit(solution)/shard_map/ppermute | solution.py:10
  36.6 17.7 %collective-permute-start.4 = (f32[2,64,128]{2,1,0:T(8,128)S(1)}, f32[2,64,128]{2,1,0:T(8,128)S(1)}, u32[]{:S(2)}, u32[]{:S(2)}) collective-permute-start(f32[2,64,128]{2,1,0:T(8,128)S(1)} %maximum_add_fusion.3), channel_id=1, source_target_pairs={{0,16},{1,17},{2,18},{3,19},{4,20},{5,21},{6,22},{7,23},{8,24},{9,... | collective-permute-start | bytes 196616 | tf_op jit(solution)/shard_map/ppermute | solution.py:10
  42.4 7.0 %copy-start.1 = (f32[8,2,256,256]{3,2,1,0:T(8,128)S(1)}, f32[8,2,256,256]{3,2,1,0:T(8,128)}, u32[]{:S(2)}) copy-start(f32[8,2,256,256]{3,2,1,0:T(8,128)} %param.17) | copy-start | bytes 12582916
  54.6 25.8 %copy-start.3 = (f32[16,2,64,256]{3,2,1,0:T(8,128)S(1)}, f32[16,2,64,256]{3,2,1,0:T(8,128)}, u32[]{:S(2)}) copy-start(f32[16,2,64,256]{3,2,1,0:T(8,128)} %param.14) | copy-start | bytes 6291460
  55.5 4.4 %collective-permute-start.5 = (f32[2,64,128]{2,1,0:T(8,128)S(1)}, f32[2,64,128]{2,1,0:T(8,128)S(1)}, u32[]{:S(2)}, u32[]{:S(2)}) collective-permute-start(f32[2,64,128]{2,1,0:T(8,128)S(1)} %maximum_add_fusion.4), channel_id=1, source_target_pairs={{0,32},{1,33},{2,34},{3,35},{4,36},{5,37},{6,38},{7,39},{8,40},{9,... | collective-permute-start | bytes 196616 | tf_op jit(solution)/shard_map/ppermute | solution.py:10
  61.0 7.2 %collective-permute-start.6 = (f32[2,64,128]{2,1,0:T(8,128)S(1)}, f32[2,64,128]{2,1,0:T(8,128)S(1)}, u32[]{:S(2)}, u32[]{:S(2)}) collective-permute-start(f32[2,64,128]{2,1,0:T(8,128)S(1)} %maximum_add_fusion.5), channel_id=1, source_target_pairs={{0,64},{1,65},{2,66},{3,67},{4,68},{5,69},{6,70},{7,71},{8,72},{9,... | collective-permute-start | bytes 196616 | tf_op jit(solution)/shard_map/ppermute | solution.py:10
  69.4 9.9 %collective-permute-start.7 = (f32[2,64,128]{2,1,0:T(8,128)S(1)}, f32[2,64,128]{2,1,0:T(8,128)S(1)}, u32[]{:S(2)}, u32[]{:S(2)}) collective-permute-start(f32[2,64,128]{2,1,0:T(8,128)S(1)} %maximum_add_fusion.6), channel_id=1, source_target_pairs={{0,128},{1,129},{2,130},{3,131},{4,132},{5,133},{6,134},{7,135},{8... | collective-permute-start | bytes 196616 | tf_op jit(solution)/shard_map/ppermute | solution.py:10
where the time goes:
time: 83.8 us; the launch traced here: 83.6 us
  matrix products  33.3 us (40%)
  starting transfers between devices  27.9 us (33%)
  waiting for transfers between devices  17.8 us (21%)
  local copies, waits for them, and re-layouts  2.09 us (2%)
  between operations  1.5 us (2%)
  other arithmetic  1.02 us (1%)
    ppermute x8, starting transfers between devices, from_partner(): lax.ppermute(x, axis, [(i, i ^ 1 << bit) for i in range(lax.axis_size(axi...  23.4 us
    ppermute x8, waiting for transfers between devices, from_partner(): lax.ppermute(x, axis, [(i, i ^ 1 << bit) for i in range(lax.axis_size(axi...  17.8 us
    dot_general x16, matrix products, apply_block(): jnp.dot(w_imag, panel[1], precision=HIGH, preferred_element_type=jnp.floa...  3.7 us
    dot_general x16, matrix products, apply_block(): jnp.dot(w_imag, panel[0], precision=HIGH, preferred_element_type=jnp.floa...  3.7 us
    dot_general x1, matrix products, body(): jnp.einsum('bpq,bsq->bsp', near_blocks[:, 1], picked[0], precision=HIGH)  3.54 us
    dot_general x1, matrix products, body(): jnp.einsum('bpq,bsq->bsp', near_blocks[:, 0], picked[1], precision=HIGH)  3.4 us
    dot_general x16, matrix products, apply_block(): jnp.dot(w_real, panel[1], precision=HIGH, preferred_element_type=jnp.floa...  2.76 us
    dot_general x16, matrix products, apply_block(): jnp.dot(w_real, panel[0], precision=HIGH, preferred_element_type=jnp.floa...  2.76 us
  transfers between devices with their start and end apart: 10, of which 6 were waited for; matrix products, arithmetic and copies ran while one was open for 34% of the time, Pallas kernels for 0%

commit v1 on v0

v1 whole, which is shorter than its diff:
```python
import functools

import jax
import jax.numpy as jnp
from jax import lax
from jax.experimental import pallas as pl
from jax.experimental.pallas import tpu as pltpu
from jax.sharding import PartitionSpec as P

MESH = pl.DeviceIdType.MESH
F32, BF16 = jnp.float32, jnp.bfloat16
GROUPS = ((0,), (1, 2), (3, 4), (5,), (6, 7))
CHUNKS = 2
HALO = 4


def masks_of(group):
    if len(group) == 1:
        return (1 << group[0],)
    low, high = 1 << group[0], 1 << group[1]
    return (low, high, low | high)


MASKS = tuple(masks_of(g) for g in GROUPS)
FIRST = tuple(sum(len(m) for m in MASKS[:i]) for i in range(len(MASKS)))
N_RECV = sum(len(m) for m in MASKS)
W_FIRST = tuple(sum(len(m) + 1 for m in MASKS[:i]) for i in range(len(MASKS)))
N_W = N_RECV + len(MASKS)
DOUBLE = tuple(i for i, g in enumerate(GROUPS) if len(g) == 2)


def split(x):
    high = x.astype(BF16)
    return high, (x - high.astype(F32)).astype(BF16)


def dot(a, b):
    return jnp.dot(a, b, preferred_element_type=F32)


def dot_nt(a, b):
    return lax.dot_general(a, b, (((1,), (1,)), ((), ())), preferred_element_type=F32)


def kernel(src_hbm, slot_hbm, inb_hbm, bf_hbm, outb_hbm, pairs_hbm, count_hbm, near_hbm, out_ref,
           src, inb, bf, outb, near, slots, pairs, count, bp, pack, halo, w, wtmp, obf, nacc, panel, recv,
           load_sem, in_sem, bp_send, bp_recv, halo_send, halo_recv, p_send, p_recv):
    n = lax.axis_size("leaf")
    me = lax.axis_index("leaf")
    nxt, prv = lax.rem(me + 1, n), lax.rem(me + n - 1, n)
    leaves = src.shape[1]
    base = me * leaves
    rows = panel.shape[1]
    part = rows // CHUNKS
    rank2 = panel.shape[2]
    rank = rank2 // 2

    barrier = pltpu.get_barrier_semaphore()
    partners = [me ^ m for ms in MASKS for m in ms] + [nxt, prv]
    for p in partners:
        pl.semaphore_signal(barrier, inc=1, device_id=(p,), device_id_type=MESH)

    loads = [
        pltpu.make_async_copy(bf_hbm, bf, load_sem.at[0]),
        pltpu.make_async_copy(src_hbm, src, load_sem.at[1]),
        pltpu.make_async_copy(slot_hbm, slots, load_sem.at[2]),
        pltpu.make_async_copy(pairs_hbm, pairs, load_sem.at[3]),
        pltpu.make_async_copy(count_hbm, count, load_sem.at[4]),
        pltpu.make_async_copy(outb_hbm, outb, load_sem.at[5]),
        pltpu.make_async_copy(near_hbm, near, load_sem.at[6]),
    ]
    per = leaves // in_sem.shape[0]
    in_loads = [
        pltpu.make_async_copy(inb_hbm.at[pl.ds(i * per, per)], inb.at[pl.ds(i * per, per)], in_sem.at[i])
        for i in range(in_sem.shape[0])
    ]
    for c in loads[:2] + in_loads + loads[2:]:
        c.start()

    lane = lax.broadcasted_iota(jnp.int32, (1, rank2), 1)
    sign = jnp.where(lane < rank, 1.0, -1.0).astype(F32)

    def real_form(block):
        return jnp.concatenate([block * sign, pltpu.roll(block, rank, 1)], axis=0).T

    def weights(t):
        row = jnp.concatenate(split(t), axis=1)
        return jnp.concatenate([row, row], axis=0)

    def times(x, wide):
        y = dot(jnp.concatenate(split(x), axis=1), wide)
        return y[:, :rank2] + y[:, rank2:]

    def prepare_single(i):
        b = GROUPS[i][0]
        for k in range(2):
            w[W_FIRST[i] + k] = weights(real_form(bf[2 * b + k]))

    def prepare_double(i):
        a, b = GROUPS[i]
        d = DOUBLE.index(i)
        for k in range(2):
            if k == 0:
                lower = [bf[2 * a], bf[2 * a + 1]]
            else:
                bp_copy[d].wait_recv()
                lower = [bp[d, 0], bp[d, 1]]
            wtmp[...] = weights(real_form(bf[2 * b + k]))
            t = times(jnp.concatenate([real_form(x) for x in lower], axis=0), wtmp[...])
            w[W_FIRST[i] + 2 * k] = weights(t[:rank2])
            w[W_FIRST[i] + 2 * k + 1] = weights(t[rank2:])

    def panel_copies(i, c):
        sl = pl.ds(c * part, part)
        return [
            pltpu.make_async_remote_copy(
                src_ref=panel.at[i, sl], dst_ref=recv.at[FIRST[i] + e, sl],
                send_sem=p_send.at[FIRST[i] + e, c], recv_sem=p_recv.at[FIRST[i] + e, c],
                device_id=(me ^ m,), device_id_type=MESH)
            for e, m in enumerate(MASKS[i])
        ]

    copies = [[panel_copies(i, c) for c in range(CHUNKS)] for i in range(len(GROUPS))]
    bp_copy = [
        pltpu.make_async_remote_copy(
            src_ref=bf.at[pl.ds(2 * GROUPS[i][0], 2)], dst_ref=bp.at[d],
            send_sem=bp_send.at[d], recv_sem=bp_recv.at[d],
            device_id=(me ^ (1 << GROUPS[i][1]),), device_id_type=MESH)
        for d, i in enumerate(DOUBLE)
    ]
    halo_copy = [
        pltpu.make_async_remote_copy(
            src_ref=pack.at[pl.ds(h * HALO, HALO)], dst_ref=halo.at[pl.ds(h * HALO, HALO)],
            send_sem=halo_send.at[h], recv_sem=halo_recv.at[h], device_id=(to,), device_id_type=MESH)
        for h, to in ((0, nxt), (1, prv))
    ]

    loads[0].wait()
    prepare_single(0)
    loads[1].wait()

    def coeff(j, carry):
        x = jnp.concatenate([src[0, j], src[1, j]], axis=0)
        y = dot_nt(jnp.concatenate(split(x), axis=0), jnp.concatenate(split(inb[j]), axis=0))
        y = y[:16] + y[16:]
        y = y[:, :rank2] + y[:, rank2:]
        panel[0, pl.ds(pl.multiple_of(j * 8, 8), 8)] = y[:8] - sign * pltpu.roll(y[8:], rank, 1)
        return carry

    waited = 0
    for c in range(CHUNKS):
        count_in = (c + 1) * len(in_loads) // CHUNKS
        for i in range(waited, count_in):
            in_loads[i].wait()
            lax.fori_loop(i * per, (i + 1) * per, coeff, 0, unroll=True)
        waited = count_in
        if c == 0:
            pl.semaphore_wait(barrier, len(partners))
        for cp in copies[0][c]:
            cp.start()

    for cp in bp_copy:
        cp.start()
    loads[2].wait()
    for h in range(2):
        for i in range(HALO):
            leaf = base + (leaves - HALO + i if h == 0 else i)
            where = jnp.clip(slots[leaf] - base, 0, leaves - 1)
            pack[h * HALO + i] = src[:, where]
        halo_copy[h].start()

    def prepare_out(j, carry):
        high, low = split(outb[j])
        obf[j, pl.ds(0, rank2)] = high
        obf[j, pl.ds(rank2, rank2)] = low
        return carry

    leaf_iota = lax.broadcasted_iota(jnp.int32, (leaves, 1, 1), 0)

    def near_term(k, carry):
        a, t = pairs[0, k], pairs[1, k]
        own = jnp.clip(slots[a] - base, 0, leaves - 1)
        off = jnp.clip(jnp.where(a < base, a - base + HALO, a - base - leaves + HALO), 0, 2 * HALO - 1)
        inside = jnp.logical_and(a >= base, a < base + leaves)
        x = jnp.where(inside, src[:, own], halo[off]).reshape(16, -1)
        high, low = split(x)
        both = jnp.concatenate([high, low], axis=0)
        y = []
        for q in range(2):
            bh, bl = split(near[k, q])
            yh, yl = dot_nt(both, bh), dot_nt(high, bl)
            y.append(yh[:16] + yh[16:] + yl)
        hit = jnp.logical_and(leaf_iota == slots[t] - base, k < count[0])
        nacc[0] += jnp.where(hit, (y[0][:8] - y[1][8:])[None], 0.0)
        nacc[1] += jnp.where(hit, (y[0][8:] + y[1][:8])[None], 0.0)
        return carry

    def background(i):
        if i == 0:
            prepare_single(3)
            loads[5].wait()
            lax.fori_loop(0, leaves // 4, prepare_out, 0)
        if i == 1:
            prepare_double(1)
            prepare_double(2)
        if i == 2:
            prepare_double(4)
            lax.fori_loop(leaves // 4, leaves, prepare_out, 0)
            loads[3].wait()
            loads[4].wait()
            loads[6].wait()
            nacc[...] = jnp.zeros_like(nacc)
            for cp in halo_copy:
                cp.wait_recv()
        if i == 3:
            lax.fori_loop(0, 3, near_term, 0)
        if i == 4:
            lax.fori_loop(3, 8, near_term, 0)

    last = len(GROUPS) - 1
    for i in range(len(GROUPS)):
        own = [None] * CHUNKS
        if i in (0, 3):
            own = [times(panel[i, pl.ds(c * part, part)], w[W_FIRST[i]]) for c in range(CHUNKS)]
        background(i)
        if i not in (0, 3):
            own = [times(panel[i, pl.ds(c * part, part)], w[W_FIRST[i]]) for c in range(CHUNKS)]
        for c in range(CHUNKS):
            sl = pl.ds(c * part, part)
            acc = own[c]
            for e, cp in enumerate(copies[i][c]):
                cp.wait_recv()
                acc = acc + times(recv[FIRST[i] + e, sl], w[W_FIRST[i] + 1 + e])
            if i < last:
                panel[i + 1, sl] = acc
                for cp in copies[i + 1][c]:
                    cp.start()
            else:
                for j in range(c * leaves // CHUNKS, (c + 1) * leaves // CHUNKS):
                    r = (j - c * leaves // CHUNKS) * 8
                    x = acc[r:r + 8]
                    high, low = split(jnp.concatenate([x * sign, pltpu.roll(x, rank, 1)], axis=0))
                    lhs = jnp.concatenate(
                        [jnp.concatenate([high, high], axis=1), jnp.concatenate([low, low], axis=1)], axis=0)
                    y = dot(lhs, obf[j])
                    y = y[:16] + y[16:]
                    out_ref[0, j] = y[:8] + nacc[0, j]
                    out_ref[1, j] = y[8:] + nacc[1, j]

    for row in copies:
        for chunk in row:
            for cp in chunk:
                cp.wait_send()
    for cp in bp_copy + halo_copy:
        cp.wait_send()


def body(sources, leaf_slot, in_basis, butterfly, out_basis, near_pairs, near_count, near_blocks):
    leaves, s, size = sources.shape[1:]
    rank = in_basis.shape[2]
    levels = butterfly.shape[0]
    slots = near_pairs.shape[0]
    rows = leaves * s
    any_spec = pl.BlockSpec(memory_space=pl.ANY)
    dma = pltpu.SemaphoreType.DMA
    return pl.pallas_call(
        kernel,
        out_shape=pltpu.VMEM(sources.shape, F32),
        in_specs=[any_spec] * 8,
        out_specs=pl.BlockSpec(memory_space=pltpu.VMEM),
        scratch_shapes=[
            pltpu.VMEM(sources.shape, F32),
            pltpu.VMEM((leaves, 2 * rank, size), F32),
            pltpu.VMEM((2 * levels, rank, 2 * rank), F32),
            pltpu.VMEM((leaves, 2 * rank, size), F32),
            pltpu.VMEM(near_blocks.shape, F32),
            pltpu.SMEM(leaf_slot.shape, jnp.int32),
            pltpu.SMEM(near_pairs.shape[::-1], jnp.int32),
            pltpu.SMEM(near_count.shape, jnp.int32),
            pltpu.VMEM((len(DOUBLE), 2, rank, 2 * rank), F32),
            pltpu.VMEM((2 * HALO, 2, s, size), F32),
            pltpu.VMEM((2 * HALO, 2, s, size), F32),
            pltpu.VMEM((N_W, 4 * rank, 4 * rank), BF16),
            pltpu.VMEM((4 * rank, 4 * rank), BF16),
            pltpu.VMEM((leaves, 4 * rank, size), BF16),
            pltpu.VMEM(sources.shape, F32),
            pltpu.VMEM((len(GROUPS), rows, 2 * rank), F32),
            pltpu.VMEM((N_RECV, rows, 2 * rank), F32),
            dma((7,)),
            dma((4,)),
            dma((len(DOUBLE),)),
            dma((len(DOUBLE),)),
            dma((2,)),
            dma((2,)),
            dma((N_RECV, CHUNKS)),
            dma((N_RECV, CHUNKS)),
        ],
        compiler_params=pltpu.CompilerParams(
            collective_id=0, has_side_effects=True, vmem_limit_bytes=60 * 1024 * 1024),
        name="butterfly",
    )(sources, leaf_slot, in_basis.reshape(leaves, 2 * rank, size),
      butterfly.reshape(2 * levels, rank, 2 * rank), out_basis.reshape(leaves, 2 * rank, size),
      near_pairs.T, near_count, near_blocks)


def solution(mesh):
    in_specs = (
        P(None, "leaf", None, None),
        P(),
        P("leaf", None, None, None),
        P(None, "leaf", None, None, None),
        P("leaf", None, None, None),
        P("leaf", None),
        P("leaf"),
        P("leaf", None, None, None),
    )
    out_specs = P(None, "leaf", None, None)
    return jax.shard_map(body, mesh=mesh, in_specs=in_specs, out_specs=out_specs, check_vma=False)
```

time: 83.8 us -> 33.7 us (0.40)
  the two profiles are of different devices: /device:TPU:26 before, /device:TPU:8 now
where the time goes in v1:
time: 33.7 us; the launch traced here: 33.6 us
  Pallas kernels  32.2 us (96%)
  local copies, waits for them, and re-layouts  0.71 us (2%)
  between operations  0.66 us (2%)
    pallas_call x1, Pallas kernels, body(): pl.pallas_call(kernel, out_shape=pltpu.VMEM(sources.shape, F32), in_specs...  32.2 us
    unnamed x1, local copies, waits for them, and re-layouts  0.71 us

profile of v1, /device:TPU:8, one launch (start us, length us, event | category | flops | bytes accessed | tf_op | source)
XLA Modules:
  0.0 33.6 jit_solution(1408579722421082386)
XLA Ops:
  0.7 32.2 %butterfly.1 = f32[2,16,8,256]{3,2,1,0:T(8,128)S(1)} custom-call(f32[2,16,8,256]{3,2,1,0:T(8,128)} %src_hbm.1, s32[4096]{0:T(1024)} %slot_hbm.1, f32[16,128,256]{2,1,0:T(8,128)} %bitcast.4, f32[16,64,128]{2,1,0:T(8,128)} %bitcast.6, f32[16,128,256]{2,1,0:T(8,128)} %bitcast.5, s32[2,8]{1,0:T(2,128)} %bitcast.7, s32[1]{0:T(128)S(6)} %copy.11.count_hbm, ...), custom_call_target="tpu_custom_call" | custom-call | tf_op jit(solution)/shard_map/butterfly/pallas_call | solution.py:266
  32.9 0.7 %copy.10 = f32[2,16,8,256]{3,2,1,0:T(8,128)} copy(f32[2,16,8,256]{3,2,1,0:T(8,128)S(1)} %butterfly.1) | data formatting | bytes 524288

commit v2 on v1

--- a/solution.py
+++ b/solution.py
@@ -10,7 +10,9 @@
 MESH = pl.DeviceIdType.MESH
 F32, BF16 = jnp.float32, jnp.bfloat16
 GROUPS = ((0,), (1, 2), (3, 4), (5,), (6, 7))
-CHUNKS = 2
+CHUNK_LEAVES = (4, 4, 4, 4)
+CHUNKS = len(CHUNK_LEAVES)
+START = tuple(sum(CHUNK_LEAVES[:c]) for c in range(CHUNKS + 1))
 HALO = 4
 
 
@@ -44,20 +46,21 @@
 
 def kernel(src_hbm, slot_hbm, inb_hbm, bf_hbm, outb_hbm, pairs_hbm, count_hbm, near_hbm, out_ref,
            src, inb, bf, outb, near, slots, pairs, count, bp, pack, halo, w, wtmp, obf, nacc, panel, recv,
-           load_sem, in_sem, bp_send, bp_recv, halo_send, halo_recv, p_send, p_recv):
+           load_sem, in_sem, bp_send, bp_recv, halo_send, halo_recv, p_send, p_recv, known):
     n = lax.axis_size("leaf")
     me = lax.axis_index("leaf")
     nxt, prv = lax.rem(me + 1, n), lax.rem(me + n - 1, n)
     leaves = src.shape[1]
     base = me * leaves
-    rows = panel.shape[1]
-    part = rows // CHUNKS
+    width = panel.shape[1] // leaves
     rank2 = panel.shape[2]
     rank = rank2 // 2
 
+    step = 1 << GROUPS[3][0]
+    up, down = lax.rem(me + step, n), lax.rem(me + n - step, n)
     barrier = pltpu.get_barrier_semaphore()
-    partners = [me ^ m for ms in MASKS for m in ms] + [nxt, prv]
-    for p in partners:
+    neighbours = [me ^ 1, me ^ 2, me ^ 4, me ^ 6, me ^ 8, me ^ 16, me ^ 24, up, down, nxt, prv]
+    for p in neighbours:
         pl.semaphore_signal(barrier, inc=1, device_id=(p,), device_id_type=MESH)
 
     loads = [
@@ -74,7 +77,7 @@
         pltpu.make_async_copy(inb_hbm.at[pl.ds(i * per, per)], inb.at[pl.ds(i * per, per)], in_sem.at[i])
         for i in range(in_sem.shape[0])
     ]
-    for c in loads[:2] + in_loads + loads[2:]:
+    for c in [loads[0], loads[1]] + in_loads + loads[2:]:
         c.start()
 
     lane = lax.broadcasted_iota(jnp.int32, (1, rank2), 1)
@@ -84,12 +87,13 @@
         return jnp.concatenate([block * sign, pltpu.roll(block, rank, 1)], axis=0).T
 
     def weights(t):
-        row = jnp.concatenate(split(t), axis=1)
-        return jnp.concatenate([row, row], axis=0)
-
-    def times(x, wide):
-        y = dot(jnp.concatenate(split(x), axis=1), wide)
-        return y[:, :rank2] + y[:, rank2:]
+        return jnp.concatenate(split(t), axis=1)
+
+    def times(xs, wide):
+        high, low = zip(*[split(x) for x in xs])
+        y = dot(jnp.concatenate([jnp.concatenate(high, axis=1), jnp.concatenate(low, axis=1)], axis=0), wide)
+        y = y[:, :rank2] + y[:, rank2:]
+        return y[:y.shape[0] // 2] + y[y.shape[0] // 2:]
 
     def prepare_single(i):
         b = GROUPS[i][0]
@@ -106,37 +110,51 @@
                 bp_copy[d].wait_recv()
                 lower = [bp[d, 0], bp[d, 1]]
             wtmp[...] = weights(real_form(bf[2 * b + k]))
-            t = times(jnp.concatenate([real_form(x) for x in lower], axis=0), wtmp[...])
+            t = times([jnp.concatenate([real_form(x) for x in lower], axis=0)], wtmp[...])
             w[W_FIRST[i] + 2 * k] = weights(t[:rank2])
             w[W_FIRST[i] + 2 * k + 1] = weights(t[rank2:])
 
+    def chunk(c):
+        return pl.ds(START[c] * width, CHUNK_LEAVES[c] * width)
+
     def panel_copies(i, c):
-        sl = pl.ds(c * part, part)
         return [
             pltpu.make_async_remote_copy(
-                src_ref=panel.at[i, sl], dst_ref=recv.at[FIRST[i] + e, sl],
-                send_sem=p_send.at[FIRST[i] + e, c], recv_sem=p_recv.at[FIRST[i] + e, c],
+                src_ref=panel.at[i, chunk(c)], dst_ref=recv.at[FIRST[i] + e, chunk(c)],
+                send_sem=p_send.at[0], recv_sem=p_recv.at[i, c],
                 device_id=(me ^ m,), device_id_type=MESH)
             for e, m in enumerate(MASKS[i])
         ]
 
-    copies = [[panel_copies(i, c) for c in range(CHUNKS)] for i in range(len(GROUPS))]
+    def send(i, c):
+        for cp in panel_copies(i, c)[::-1]:
+            cp.start()
+
+    def arrive(i, c):
+        ref = recv.at[pl.ds(FIRST[i], len(MASKS[i])), chunk(c)]
+        pltpu.make_async_copy(ref, ref, p_recv.at[i, c]).wait()
+
     bp_copy = [
         pltpu.make_async_remote_copy(
             src_ref=bf.at[pl.ds(2 * GROUPS[i][0], 2)], dst_ref=bp.at[d],
-            send_sem=bp_send.at[d], recv_sem=bp_recv.at[d],
+            send_sem=bp_send.at[0], recv_sem=bp_recv.at[d],
             device_id=(me ^ (1 << GROUPS[i][1]),), device_id_type=MESH)
         for d, i in enumerate(DOUBLE)
     ]
     halo_copy = [
         pltpu.make_async_remote_copy(
             src_ref=pack.at[pl.ds(h * HALO, HALO)], dst_ref=halo.at[pl.ds(h * HALO, HALO)],
-            send_sem=halo_send.at[h], recv_sem=halo_recv.at[h], device_id=(to,), device_id_type=MESH)
+            send_sem=halo_send.at[0], recv_sem=halo_recv.at[h], device_id=(to,), device_id_type=MESH)
         for h, to in ((0, nxt), (1, prv))
     ]
 
+    def tell(k, to):
+        pl.semaphore_signal(known.at[k], inc=1, device_id=(to,), device_id_type=MESH)
+
     loads[0].wait()
-    prepare_single(0)
+    pl.semaphore_wait(barrier, len(neighbours))
+    bp_copy[0].start()
+    bp_copy[1].start()
     loads[1].wait()
 
     def coeff(j, carry):
@@ -149,25 +167,25 @@
 
     waited = 0
     for c in range(CHUNKS):
-        count_in = (c + 1) * len(in_loads) // CHUNKS
+        count_in = -(-START[c + 1] // per)
         for i in range(waited, count_in):
             in_loads[i].wait()
-            lax.fori_loop(i * per, (i + 1) * per, coeff, 0, unroll=True)
         waited = count_in
-        if c == 0:
-            pl.semaphore_wait(barrier, len(partners))
-        for cp in copies[0][c]:
-            cp.start()
-
-    for cp in bp_copy:
-        cp.start()
-    loads[2].wait()
-    for h in range(2):
-        for i in range(HALO):
-            leaf = base + (leaves - HALO + i if h == 0 else i)
-            where = jnp.clip(slots[leaf] - base, 0, leaves - 1)
-            pack[h * HALO + i] = src[:, where]
-        halo_copy[h].start()
+        lax.fori_loop(START[c], START[c + 1], coeff, 0, unroll=True)
+        send(0, c)
+
+    tell(2, up)
+    tell(2, down)
+    prepare_single(0)
+
+    def pack_halo():
+        loads[2].wait()
+        for h in range(2):
+            for i in range(HALO):
+                leaf = base + (leaves - HALO + i if h == 0 else i)
+                where = jnp.clip(slots[leaf] - base, 0, leaves - 1)
+                pack[h * HALO + i] = src[:, where]
+            halo_copy[h].start()
 
     def prepare_out(j, carry):
         high, low = split(outb[j])
@@ -198,61 +216,54 @@
     def background(i):
         if i == 0:
             prepare_single(3)
-            loads[5].wait()
-            lax.fori_loop(0, leaves // 4, prepare_out, 0)
+            pl.semaphore_wait(known.at[2], 2)
+            tell(3, me ^ (1 << GROUPS[4][0]))
         if i == 1:
             prepare_double(1)
             prepare_double(2)
         if i == 2:
+            pl.semaphore_wait(known.at[3], 1)
+            bp_copy[2].start()
+            pack_halo()
+            loads[5].wait()
+            lax.fori_loop(0, leaves, prepare_out, 0)
+        if i == 4:
             prepare_double(4)
-            lax.fori_loop(leaves // 4, leaves, prepare_out, 0)
             loads[3].wait()
             loads[4].wait()
             loads[6].wait()
             nacc[...] = jnp.zeros_like(nacc)
             for cp in halo_copy:
                 cp.wait_recv()
-        if i == 3:
-            lax.fori_loop(0, 3, near_term, 0)
-        if i == 4:
-            lax.fori_loop(3, 8, near_term, 0)
+            lax.fori_loop(0, 8, near_term, 0)
+
+    def far(acc, j, r):
+        x = acc[r:r + width]
+        high, low = split(jnp.concatenate([x * sign, pltpu.roll(x, rank, 1)], axis=0))
+        lhs = jnp.concatenate(
+            [jnp.concatenate([high, high], axis=1), jnp.concatenate([low, low], axis=1)], axis=0)
+        y = dot(lhs, obf[j])
+        y = y[:16] + y[16:]
+        out_ref[0, j] = y[:8] + nacc[0, j]
+        out_ref[1, j] = y[8:] + nacc[1, j]
 
     last = len(GROUPS) - 1
     for i in range(len(GROUPS)):
-        own = [None] * CHUNKS
-        if i in (0, 3):
-            own = [times(panel[i, pl.ds(c * part, part)], w[W_FIRST[i]]) for c in range(CHUNKS)]
         background(i)
-        if i not in (0, 3):
-            own = [times(panel[i, pl.ds(c * part, part)], w[W_FIRST[i]]) for c in range(CHUNKS)]
+        blocks = len(MASKS[i]) + 1
         for c in range(CHUNKS):
-            sl = pl.ds(c * part, part)
-            acc = own[c]
-            for e, cp in enumerate(copies[i][c]):
-                cp.wait_recv()
-                acc = acc + times(recv[FIRST[i] + e, sl], w[W_FIRST[i] + 1 + e])
+            arrive(i, c)
+            xs = [panel[i, chunk(c)]] + [recv[FIRST[i] + e, chunk(c)] for e in range(blocks - 1)]
+            acc = times(xs, w[pl.ds(W_FIRST[i], blocks)].reshape(blocks * rank2, 2 * rank2))
             if i < last:
-                panel[i + 1, sl] = acc
-                for cp in copies[i + 1][c]:
-                    cp.start()
+                panel[i + 1, chunk(c)] = acc
+                send(i + 1, c)
             else:
-                for j in range(c * leaves // CHUNKS, (c + 1) * leaves // CHUNKS):
-                    r = (j - c * leaves // CHUNKS) * 8
-                    x = acc[r:r + 8]
-                    high, low = split(jnp.concatenate([x * sign, pltpu.roll(x, rank, 1)], axis=0))
-                    lhs = jnp.concatenate(
-                        [jnp.concatenate([high, high], axis=1), jnp.concatenate([low, low], axis=1)], axis=0)
-                    y = dot(lhs, obf[j])
-                    y = y[:16] + y[16:]
-                    out_ref[0, j] = y[:8] + nacc[0, j]
-                    out_ref[1, j] = y[8:] + nacc[1, j]
-
-    for row in copies:
-        for chunk in row:
-            for cp in chunk:
-                cp.wait_send()
-    for cp in bp_copy + halo_copy:
-        cp.wait_send()
+                for j in range(START[c], START[c + 1]):
+                    far(acc, j, (j - START[c]) * width)
+
+    for ref, sem in ((recv, p_send), (bp, bp_send), (pack, halo_send)):
+        pltpu.make_async_copy(ref, ref, sem.at[0]).wait()
 
 
 def body(sources, leaf_slot, in_basis, butterfly, out_basis, near_pairs, near_count, near_blocks):
@@ -261,7 +272,7 @@
     levels = butterfly.shape[0]
     slots = near_pairs.shape[0]
     rows = leaves * s
-    any_spec = pl.BlockSpec(memory_space=pl.ANY)
+    any_spec = pl.BlockSpec(memory_space=pltpu.HBM)
     dma = pltpu.SemaphoreType.DMA
     return pl.pallas_call(
         kernel,
@@ -280,20 +291,21 @@
             pltpu.VMEM((len(DOUBLE), 2, rank, 2 * rank), F32),
             pltpu.VMEM((2 * HALO, 2, s, size), F32),
             pltpu.VMEM((2 * HALO, 2, s, size), F32),
-            pltpu.VMEM((N_W, 4 * rank, 4 * rank), BF16),
-            pltpu.VMEM((4 * rank, 4 * rank), BF16),
+            pltpu.VMEM((N_W, 2 * rank, 4 * rank), BF16),
+            pltpu.VMEM((2 * rank, 4 * rank), BF16),
             pltpu.VMEM((leaves, 4 * rank, size), BF16),
             pltpu.VMEM(sources.shape, F32),
             pltpu.VMEM((len(GROUPS), rows, 2 * rank), F32),
             pltpu.VMEM((N_RECV, rows, 2 * rank), F32),
             dma((7,)),
             dma((4,)),
+            dma((1,)),
             dma((len(DOUBLE),)),
-            dma((len(DOUBLE),)),
+            dma((1,)),
             dma((2,)),
-            dma((2,)),
-            dma((N_RECV, CHUNKS)),
-            dma((N_RECV, CHUNKS)),
+            dma((1,)),
+            dma((len(GROUPS), CHUNKS)),
+            pltpu.SemaphoreType.REGULAR((4,)),
         ],
         compiler_params=pltpu.CompilerParams(
             collective_id=0, has_side_effects=True, vmem_limit_bytes=60 * 1024 * 1024),

time: 33.7 us -> 31.5 us (0.935)
  Pallas kernels: 32.2 us -> 29.7 us
    pallas_call x1, Pallas kernels: 32.2 us -> 29.7 us  [body(): pl.pallas_call(kernel, out_shape=pltpu.VMEM(sources.shape, F32), in_specs...]
where the time goes in v2:
time: 31.5 us; the launch traced here: 31.1 us
  Pallas kernels  29.7 us (94%)
  local copies, waits for them, and re-layouts  0.71 us (2%)
  between operations  0.66 us (2%)
    pallas_call x1, Pallas kernels, body(): pl.pallas_call(kernel, out_shape=pltpu.VMEM(sources.shape, F32), in_specs...  29.7 us
    unnamed x1, local copies, waits for them, and re-layouts  0.71 us

profile of v2, /device:TPU:8, one launch (start us, length us, event | category | flops | bytes accessed | tf_op | source)
XLA Modules:
  0.0 31.1 jit_solution(9246044022705198166)
XLA Ops:
  0.7 29.7 %butterfly.1 = f32[2,16,8,256]{3,2,1,0:T(8,128)S(1)} custom-call(f32[2,16,8,256]{3,2,1,0:T(8,128)} %src_hbm.1, s32[4096]{0:T(1024)} %slot_hbm.1, f32[16,128,256]{2,1,0:T(8,128)} %bitcast.4, f32[16,64,128]{2,1,0:T(8,128)} %bitcast.6, f32[16,128,256]{2,1,0:T(8,128)} %bitcast.5, s32[2,8]{1,0:T(2,128)} %bitcast.7, s32[1]{0:T(128)S(6)} %copy.11.count_hbm, ...), custom_call_target="tpu_custom_call" | custom-call | tf_op jit(solution)/shard_map/butterfly/pallas_call | solution.py:277
  30.4 0.7 %copy.10 = f32[2,16,8,256]{3,2,1,0:T(8,128)} copy(f32[2,16,8,256]{3,2,1,0:T(8,128)S(1)} %butterfly.1) | data formatting | bytes 524288

commit v3 on v2

--- a/solution.py
+++ b/solution.py
@@ -9,9 +9,10 @@
 
 MESH = pl.DeviceIdType.MESH
 F32, BF16 = jnp.float32, jnp.bfloat16
-GROUPS = ((0,), (1, 2), (3, 4), (5,), (6, 7))
+GROUPS = ((0,), (1, 2), (3, 4))
 CHUNK_LEAVES = (4, 4, 4, 4)
 CHUNKS = len(CHUNK_LEAVES)
+DIRECT = 2
 START = tuple(sum(CHUNK_LEAVES[:c]) for c in range(CHUNKS + 1))
 HALO = 4
 
@@ -23,11 +24,13 @@
     return (low, high, low | high)
 
 
-MASKS = tuple(masks_of(g) for g in GROUPS)
+Z1, Z2 = 3, 4
+MASKS = tuple(masks_of(g) for g in GROUPS) + ((32,), (160, 128, 64, 192))
 FIRST = tuple(sum(len(m) for m in MASKS[:i]) for i in range(len(MASKS)))
 N_RECV = sum(len(m) for m in MASKS)
-W_FIRST = tuple(sum(len(m) + 1 for m in MASKS[:i]) for i in range(len(MASKS)))
-N_W = N_RECV + len(MASKS)
+W_FIRST = tuple(sum(len(m) + 1 for m in MASKS[:i]) for i in range(len(GROUPS) + 1))
+W_FAR, W_NEAR, W_OWN, W_LAST = (W_FIRST[-1] + 2 * i for i in range(4))
+N_W = W_FIRST[-1] + 8
 DOUBLE = tuple(i for i, g in enumerate(GROUPS) if len(g) == 2)
 
 
@@ -46,7 +49,8 @@
 
 def kernel(src_hbm, slot_hbm, inb_hbm, bf_hbm, outb_hbm, pairs_hbm, count_hbm, near_hbm, out_ref,
            src, inb, bf, outb, near, slots, pairs, count, bp, pack, halo, w, wtmp, obf, nacc, panel, recv,
-           load_sem, in_sem, bp_send, bp_recv, halo_send, halo_recv, p_send, p_recv, known):
+           z_panel, z_own, m_out, m_in, b_in,
+           load_sem, in_sem, bp_send, bp_recv, m_send, m_recv, halo_send, halo_recv, p_send, p_recv, known):
     n = lax.axis_size("leaf")
     me = lax.axis_index("leaf")
     nxt, prv = lax.rem(me + 1, n), lax.rem(me + n - 1, n)
@@ -56,7 +60,7 @@
     rank2 = panel.shape[2]
     rank = rank2 // 2
 
-    step = 1 << GROUPS[3][0]
+    step = MASKS[Z1][0]
     up, down = lax.rem(me + step, n), lax.rem(me + n - step, n)
     barrier = pltpu.get_barrier_semaphore()
     neighbours = [me ^ 1, me ^ 2, me ^ 4, me ^ 6, me ^ 8, me ^ 16, me ^ 24, up, down, nxt, prv]
@@ -77,7 +81,7 @@
         pltpu.make_async_copy(inb_hbm.at[pl.ds(i * per, per)], inb.at[pl.ds(i * per, per)], in_sem.at[i])
         for i in range(in_sem.shape[0])
     ]
-    for c in [loads[0], loads[1]] + in_loads + loads[2:]:
+    for c in [loads[1]] + in_loads[:1] + [loads[0]] + in_loads[1:] + loads[2:]:
         c.start()
 
     lane = lax.broadcasted_iota(jnp.int32, (1, rank2), 1)
@@ -114,24 +118,41 @@
             w[W_FIRST[i] + 2 * k] = weights(t[:rank2])
             w[W_FIRST[i] + 2 * k + 1] = weights(t[rank2:])
 
+    def prepare_z_here():
+        wtmp[...] = weights(real_form(bf[12]))
+        t = times([jnp.concatenate([real_form(bf[10]), real_form(bf[11])], axis=0)], wtmp[...])
+        w[W_FAR + 1] = weights(t[:rank2])
+        w[W_OWN] = weights(t[:rank2])
+        w[W_OWN + 1] = weights(t[rank2:])
+        m_out[...] = t[rank2:]
+        for k in range(2):
+            w[W_LAST + k] = weights(real_form(bf[14 + k]))
+
+    def prepare_z_there():
+        m_copy[0].wait_recv()
+        w[W_FAR] = weights(m_in[...])
+        m_copy[1].wait_recv()
+        wtmp[...] = weights(real_form(b_in[...]))
+        t = times([jnp.concatenate([real_form(bf[10]), real_form(bf[11])], axis=0)], wtmp[...])
+        for k in range(2):
+            w[W_NEAR + k] = weights(t[k * rank2:(k + 1) * rank2])
+
     def chunk(c):
         return pl.ds(START[c] * width, CHUNK_LEAVES[c] * width)
 
-    def panel_copies(i, c):
-        return [
-            pltpu.make_async_remote_copy(
-                src_ref=panel.at[i, chunk(c)], dst_ref=recv.at[FIRST[i] + e, chunk(c)],
-                send_sem=p_send.at[0], recv_sem=p_recv.at[i, c],
-                device_id=(me ^ m,), device_id_type=MESH)
-            for e, m in enumerate(MASKS[i])
-        ]
+    def copy_to(ref, i, e, c):
+        return pltpu.make_async_remote_copy(
+            src_ref=ref.at[chunk(c)], dst_ref=recv.at[FIRST[i] + e, chunk(c)],
+            send_sem=p_send.at[int(i == Z2 and e == 0)], recv_sem=p_recv.at[i, c],
+            device_id=(me ^ MASKS[i][e],), device_id_type=MESH)
 
     def send(i, c):
-        for cp in panel_copies(i, c)[::-1]:
-            cp.start()
+        for e in range(len(MASKS[i]))[::-1]:
+            copy_to(panel.at[i], i, e, c).start()
 
     def arrive(i, c):
-        ref = recv.at[pl.ds(FIRST[i], len(MASKS[i])), chunk(c)]
+        skip = int(i == Z2 and c < DIRECT)
+        ref = recv.at[pl.ds(FIRST[i] + skip, len(MASKS[i]) - skip), chunk(c)]
         pltpu.make_async_copy(ref, ref, p_recv.at[i, c]).wait()
 
     bp_copy = [
@@ -141,6 +162,12 @@
             device_id=(me ^ (1 << GROUPS[i][1]),), device_id_type=MESH)
         for d, i in enumerate(DOUBLE)
     ]
+    m_copy = [
+        pltpu.make_async_remote_copy(
+            src_ref=ref, dst_ref=to, send_sem=m_send.at[k], recv_sem=m_recv.at[k],
+            device_id=(me ^ m,), device_id_type=MESH)
+        for k, (ref, to, m) in enumerate(((m_out, m_in, 32), (bf.at[13], b_in, 64)))
+    ]
     halo_copy = [
         pltpu.make_async_remote_copy(
             src_ref=pack.at[pl.ds(h * HALO, HALO)], dst_ref=halo.at[pl.ds(h * HALO, HALO)],
@@ -151,10 +178,6 @@
     def tell(k, to):
         pl.semaphore_signal(known.at[k], inc=1, device_id=(to,), device_id_type=MESH)
 
-    loads[0].wait()
-    pl.semaphore_wait(barrier, len(neighbours))
-    bp_copy[0].start()
-    bp_copy[1].start()
     loads[1].wait()
 
     def coeff(j, carry):
@@ -172,7 +195,13 @@
             in_loads[i].wait()
         waited = count_in
         lax.fori_loop(START[c], START[c + 1], coeff, 0, unroll=True)
+        if c == 0:
+            pl.semaphore_wait(barrier, len(neighbours))
         send(0, c)
+        if c == 0:
+            loads[0].wait()
+            bp_copy[0].start()
+            bp_copy[1].start()
 
     tell(2, up)
     tell(2, down)
@@ -215,20 +244,23 @@
 
     def background(i):
         if i == 0:
-            prepare_single(3)
             pl.semaphore_wait(known.at[2], 2)
-            tell(3, me ^ (1 << GROUPS[4][0]))
+            tell(3, me ^ 64)
+            tell(3, me ^ 192)
         if i == 1:
             prepare_double(1)
+            prepare_z_here()
+            m_copy[0].start()
+            m_copy[1].start()
+        if i == 2:
+            pack_halo()
             prepare_double(2)
-        if i == 2:
-            pl.semaphore_wait(known.at[3], 1)
-            bp_copy[2].start()
-            pack_halo()
+            pl.semaphore_wait(known.at[3], 2)
+            prepare_z_there()
+        if i == 3:
             loads[5].wait()
             lax.fori_loop(0, leaves, prepare_out, 0)
         if i == 4:
-            prepare_double(4)
             loads[3].wait()
             loads[4].wait()
             loads[6].wait()
@@ -247,23 +279,59 @@
         out_ref[0, j] = y[:8] + nacc[0, j]
         out_ref[1, j] = y[8:] + nacc[1, j]
 
-    last = len(GROUPS) - 1
+    def stacked(first, blocks):
+        return w[pl.ds(first, blocks)].reshape(blocks * rank2, 2 * rank2)
+
+    def got(i, e, c):
+        return recv[FIRST[i] + e, chunk(c)]
+
     for i in range(len(GROUPS)):
         background(i)
         blocks = len(MASKS[i]) + 1
         for c in range(CHUNKS):
             arrive(i, c)
-            xs = [panel[i, chunk(c)]] + [recv[FIRST[i] + e, chunk(c)] for e in range(blocks - 1)]
-            acc = times(xs, w[pl.ds(W_FIRST[i], blocks)].reshape(blocks * rank2, 2 * rank2))
-            if i < last:
-                panel[i + 1, chunk(c)] = acc
-                send(i + 1, c)
-            else:
-                for j in range(START[c], START[c + 1]):
-                    far(acc, j, (j - START[c]) * width)
-
-    for ref, sem in ((recv, p_send), (bp, bp_send), (pack, halo_send)):
-        pltpu.make_async_copy(ref, ref, sem.at[0]).wait()
+            xs = [panel[i, chunk(c)]] + [got(i, e, c) for e in range(blocks - 1)]
+            acc = times(xs, stacked(W_FIRST[i], blocks))
+            panel[i + 1, chunk(c)] = acc
+            send(i + 1, c)
+            if i + 1 == Z1 and c >= DIRECT:
+                for k in (1, 0):
+                    z_panel[k, chunk(c)] = times([acc], w[W_FAR + k])
+                    copy_to(z_panel.at[k], Z2, k, c).start()
+
+    background(Z1)
+    for c in range(CHUNKS):
+        arrive(Z1, c)
+        xs = [panel[Z1, chunk(c)], got(Z1, 0, c)]
+        if c < DIRECT:
+            z_panel[1, chunk(c)] = times(xs, stacked(W_OWN, 2))
+            copy_to(z_panel.at[1], Z2, 1, c).start()
+        z_panel[2, chunk(c)] = times(xs, stacked(W_NEAR, 2))
+        for e in (2, 3):
+            copy_to(z_panel.at[2], Z2, e, c).start()
+        if c >= DIRECT:
+            z_own[chunk(c)] = times(xs, stacked(W_OWN, 2))
+
+    background(Z2)
+    for c in range(CHUNKS):
+        arrive(Z2, c)
+        here, there = z_panel[1, chunk(c)] if c < DIRECT else z_own[chunk(c)], got(Z2, 1, c) + got(Z2, 3, c)
+        if c >= DIRECT:
+            there = there + got(Z2, 0, c)
+        xs = [here + got(Z2, 2, c), there]
+        acc = times(xs, stacked(W_LAST, 2))
+        for j in range(START[c], START[c + 1]):
+            far(acc, j, (j - START[c]) * width)
+
+    for cp in m_copy:
+        cp.wait_send()
+    skipped = FIRST[Z2]
+    for ref, sem in ((recv.at[pl.ds(0, skipped)], p_send.at[0]), (recv.at[pl.ds(skipped + 1, 3)], p_send.at[0]),
+                     (bp, bp_send.at[0]), (pack, halo_send.at[0])):
+        pltpu.make_async_copy(ref, ref, sem).wait()
+    if DIRECT < CHUNKS:
+        ref = recv.at[skipped, pl.ds(START[DIRECT] * width, (leaves - START[DIRECT]) * width)]
+        pltpu.make_async_copy(ref, ref, p_send.at[1]).wait()
 
 
 def body(sources, leaf_slot, in_basis, butterfly, out_basis, near_pairs, near_count, near_blocks):
@@ -295,16 +363,23 @@
             pltpu.VMEM((2 * rank, 4 * rank), BF16),
             pltpu.VMEM((leaves, 4 * rank, size), BF16),
             pltpu.VMEM(sources.shape, F32),
-            pltpu.VMEM((len(GROUPS), rows, 2 * rank), F32),
+            pltpu.VMEM((Z1 + 1, rows, 2 * rank), F32),
             pltpu.VMEM((N_RECV, rows, 2 * rank), F32),
+            pltpu.VMEM((3, rows, 2 * rank), F32),
+            pltpu.VMEM((rows, 2 * rank), F32),
+            pltpu.VMEM((2 * rank, 2 * rank), F32),
+            pltpu.VMEM((2 * rank, 2 * rank), F32),
+            pltpu.VMEM((rank, 2 * rank), F32),
             dma((7,)),
             dma((4,)),
             dma((1,)),
             dma((len(DOUBLE),)),
+            dma((2,)),
+            dma((2,)),
             dma((1,)),
             dma((2,)),
-            dma((1,)),
-            dma((len(GROUPS), CHUNKS)),
+            dma((2,)),
+            dma((len(MASKS), CHUNKS)),
             pltpu.SemaphoreType.REGULAR((4,)),
         ],
         compiler_params=pltpu.CompilerParams(

time: 31.5 us -> 30.2 us (0.959)
  Pallas kernels: 29.7 us -> 28.5 us
    pallas_call x1, Pallas kernels: 29.7 us -> 28.5 us  [body(): pl.pallas_call(kernel, out_shape=pltpu.VMEM(sources.shape, F32), in_specs...]
where the time goes in v3:
time: 30.2 us; the launch traced here: 29.9 us
  Pallas kernels  28.5 us (94%)
  local copies, waits for them, and re-layouts  0.71 us (2%)
  between operations  0.66 us (2%)
    pallas_call x1, Pallas kernels, body(): pl.pallas_call(kernel, out_shape=pltpu.VMEM(sources.shape, F32), in_specs...  28.5 us
    unnamed x1, local copies, waits for them, and re-layouts  0.71 us

profile of v3, /device:TPU:8, one launch (start us, length us, event | category | flops | bytes accessed | tf_op | source)
XLA Modules:
  0.0 29.9 jit_solution(10992268766545940602)
XLA Ops:
  0.7 28.5 %butterfly.1 = f32[2,16,8,256]{3,2,1,0:T(8,128)S(1)} custom-call(f32[2,16,8,256]{3,2,1,0:T(8,128)} %src_hbm.1, s32[4096]{0:T(1024)} %slot_hbm.1, f32[16,128,256]{2,1,0:T(8,128)} %bitcast.4, f32[16,64,128]{2,1,0:T(8,128)} %bitcast.6, f32[16,128,256]{2,1,0:T(8,128)} %bitcast.5, s32[2,8]{1,0:T(2,128)} %bitcast.7, s32[1]{0:T(128)S(6)} %copy.11.count_hbm, ...), custom_call_target="tpu_custom_call" | custom-call | tf_op jit(solution)/shard_map/butterfly/pallas_call | solution.py:345
  29.2 0.7 %copy.10 = f32[2,16,8,256]{3,2,1,0:T(8,128)} copy(f32[2,16,8,256]{3,2,1,0:T(8,128)S(1)} %butterfly.1) | data formatting | bytes 524288

commit v4 on v3

--- a/solution.py
+++ b/solution.py
@@ -81,7 +81,7 @@
         pltpu.make_async_copy(inb_hbm.at[pl.ds(i * per, per)], inb.at[pl.ds(i * per, per)], in_sem.at[i])
         for i in range(in_sem.shape[0])
     ]
-    for c in [loads[1]] + in_loads[:1] + [loads[0]] + in_loads[1:] + loads[2:]:
+    for c in [loads[1]] + in_loads[:1] + [loads[0]] + in_loads[1:] + loads[2:5]:
         c.start()
 
     lane = lax.broadcasted_iota(jnp.int32, (1, rank2), 1)
@@ -107,20 +107,21 @@
     def prepare_double(i):
         a, b = GROUPS[i]
         d = DOUBLE.index(i)
+        for k in range(2):
+            wtmp[k] = weights(real_form(bf[2 * b + k]))
         for k in range(2):
             if k == 0:
                 lower = [bf[2 * a], bf[2 * a + 1]]
             else:
                 bp_copy[d].wait_recv()
                 lower = [bp[d, 0], bp[d, 1]]
-            wtmp[...] = weights(real_form(bf[2 * b + k]))
-            t = times([jnp.concatenate([real_form(x) for x in lower], axis=0)], wtmp[...])
+            t = times([jnp.concatenate([real_form(x) for x in lower], axis=0)], wtmp[k])
             w[W_FIRST[i] + 2 * k] = weights(t[:rank2])
             w[W_FIRST[i] + 2 * k + 1] = weights(t[rank2:])
 
     def prepare_z_here():
-        wtmp[...] = weights(real_form(bf[12]))
-        t = times([jnp.concatenate([real_form(bf[10]), real_form(bf[11])], axis=0)], wtmp[...])
+        wtmp[0] = weights(real_form(bf[12]))
+        t = times([jnp.concatenate([real_form(bf[10]), real_form(bf[11])], axis=0)], wtmp[0])
         w[W_FAR + 1] = weights(t[:rank2])
         w[W_OWN] = weights(t[:rank2])
         w[W_OWN + 1] = weights(t[rank2:])
@@ -132,8 +133,8 @@
         m_copy[0].wait_recv()
         w[W_FAR] = weights(m_in[...])
         m_copy[1].wait_recv()
-        wtmp[...] = weights(real_form(b_in[...]))
-        t = times([jnp.concatenate([real_form(bf[10]), real_form(bf[11])], axis=0)], wtmp[...])
+        wtmp[0] = weights(real_form(b_in[...]))
+        t = times([jnp.concatenate([real_form(bf[10]), real_form(bf[11])], axis=0)], wtmp[0])
         for k in range(2):
             w[W_NEAR + k] = weights(t[k * rank2:(k + 1) * rank2])
 
@@ -197,10 +198,11 @@
         lax.fori_loop(START[c], START[c + 1], coeff, 0, unroll=True)
         if c == 0:
             pl.semaphore_wait(barrier, len(neighbours))
-        send(0, c)
         if c == 0:
             loads[0].wait()
             bp_copy[0].start()
+        send(0, c)
+        if c == 0:
             bp_copy[1].start()
 
     tell(2, up)
@@ -248,11 +250,13 @@
             tell(3, me ^ 64)
             tell(3, me ^ 192)
         if i == 1:
-            prepare_double(1)
+            loads[5].start()
             prepare_z_here()
             m_copy[0].start()
             m_copy[1].start()
+            prepare_double(1)
         if i == 2:
+            loads[6].start()
             pack_halo()
             prepare_double(2)
             pl.semaphore_wait(known.at[3], 2)
@@ -360,7 +364,7 @@
             pltpu.VMEM((2 * HALO, 2, s, size), F32),
             pltpu.VMEM((2 * HALO, 2, s, size), F32),
             pltpu.VMEM((N_W, 2 * rank, 4 * rank), BF16),
-            pltpu.VMEM((2 * rank, 4 * rank), BF16),
+            pltpu.VMEM((2, 2 * rank, 4 * rank), BF16),
             pltpu.VMEM((leaves, 4 * rank, size), BF16),
             pltpu.VMEM(sources.shape, F32),
             pltpu.VMEM((Z1 + 1, rows, 2 * rank), F32),

time: 30.2 us -> 30.1 us (level)
  no operation moved by 1% of the time
where the time goes in v4:
time: 30.1 us; the launch traced here: 30 us
  Pallas kernels  28.6 us (95%)
  local copies, waits for them, and re-layouts  0.71 us (2%)
  between operations  0.66 us (2%)
    pallas_call x1, Pallas kernels, body(): pl.pallas_call(kernel, out_shape=pltpu.VMEM(sources.shape, F32), in_specs...  28.6 us
    unnamed x1, local copies, waits for them, and re-layouts  0.71 us

profile of v4, /device:TPU:8, one launch (start us, length us, event | category | flops | bytes accessed | tf_op | source)
XLA Modules:
  0.0 30.0 jit_solution(10835354342983399397)
XLA Ops:
  0.7 28.6 %butterfly.1 = f32[2,16,8,256]{3,2,1,0:T(8,128)S(1)} custom-call(f32[2,16,8,256]{3,2,1,0:T(8,128)} %src_hbm.1, s32[4096]{0:T(1024)} %slot_hbm.1, f32[16,128,256]{2,1,0:T(8,128)} %bitcast.4, f32[16,64,128]{2,1,0:T(8,128)} %bitcast.6, f32[16,128,256]{2,1,0:T(8,128)} %bitcast.5, s32[2,8]{1,0:T(2,128)} %bitcast.7, s32[1]{0:T(128)S(6)} %copy.11.count_hbm, ...), custom_call_target="tpu_custom_call" | custom-call | tf_op jit(solution)/shard_map/butterfly/pallas_call | solution.py:349
  29.3 0.7 %copy.10 = f32[2,16,8,256]{3,2,1,0:T(8,128)} copy(f32[2,16,8,256]{3,2,1,0:T(8,128)S(1)} %butterfly.1) | data formatting | bytes 524288

commit v5 on v4

--- a/solution.py
+++ b/solution.py
@@ -47,8 +47,34 @@
     return lax.dot_general(a, b, (((1,), (1,)), ((), ())), preferred_element_type=F32)
 
 
-def kernel(src_hbm, slot_hbm, inb_hbm, bf_hbm, outb_hbm, pairs_hbm, count_hbm, near_hbm, out_ref,
-           src, inb, bf, outb, near, slots, pairs, count, bp, pack, halo, w, wtmp, obf, nacc, panel, recv,
+def far_rows(x, basis):
+    rank = x.shape[1] // 2
+    sign = jnp.where(lax.broadcasted_iota(jnp.int32, (1, 2 * rank), 1) < rank, 1.0, -1.0).astype(F32)
+    high, low = split(jnp.concatenate([x * sign, pltpu.roll(x, rank, 1)], axis=0))
+    lhs = jnp.concatenate(
+        [jnp.concatenate([high, high], axis=1), jnp.concatenate([low, low], axis=1)], axis=0)
+    y = dot(lhs, basis)
+    return y[:16] + y[16:]
+
+
+def store(field, last, obf, nacc, out, tail, sem):
+    lead, each = START[-2], CHUNK_LEAVES[-1]
+    copies = [pltpu.make_async_copy(field.at[q, pl.ds(0, lead)], out.at[q, pl.ds(0, lead)], sem.at[q]) for q in range(2)]
+    for cp in copies:
+        cp.start()
+    for j in range(each):
+        y = far_rows(last[pl.ds(8 * j, 8)], obf[lead + j])
+        tail[0, j] = y[:8] + nacc[0, lead + j]
+        tail[1, j] = y[8:] + nacc[1, lead + j]
+    for q in range(2):
+        copies.append(pltpu.make_async_copy(tail.at[q], out.at[q, pl.ds(lead, each)], sem.at[2 + q]))
+        copies[-1].start()
+    for cp in copies:
+        cp.wait()
+
+
+def kernel(src_hbm, slot_hbm, inb_hbm, bf_hbm, outb_hbm, pairs_hbm, count_hbm, near_hbm, out_ref, last_ref, obf, nacc,
+           src, inb, bf, outb, near, slots, pairs, count, bp, pack, halo, w, wtmp, panel, recv,
            z_panel, z_own, m_out, m_in, b_in,
            load_sem, in_sem, bp_send, bp_recv, m_send, m_recv, halo_send, halo_recv, p_send, p_recv, known):
     n = lax.axis_size("leaf")
@@ -273,16 +299,6 @@
                 cp.wait_recv()
             lax.fori_loop(0, 8, near_term, 0)
 
-    def far(acc, j, r):
-        x = acc[r:r + width]
-        high, low = split(jnp.concatenate([x * sign, pltpu.roll(x, rank, 1)], axis=0))
-        lhs = jnp.concatenate(
-            [jnp.concatenate([high, high], axis=1), jnp.concatenate([low, low], axis=1)], axis=0)
-        y = dot(lhs, obf[j])
-        y = y[:16] + y[16:]
-        out_ref[0, j] = y[:8] + nacc[0, j]
-        out_ref[1, j] = y[8:] + nacc[1, j]
-
     def stacked(first, blocks):
         return w[pl.ds(first, blocks)].reshape(blocks * rank2, 2 * rank2)
 
@@ -324,8 +340,14 @@
             there = there + got(Z2, 0, c)
         xs = [here + got(Z2, 2, c), there]
         acc = times(xs, stacked(W_LAST, 2))
+        if c == CHUNKS - 1:
+            last_ref[...] = acc
+            continue
         for j in range(START[c], START[c + 1]):
-            far(acc, j, (j - START[c]) * width)
+            r = (j - START[c]) * width
+            y = far_rows(acc[r:r + width], obf[j])
+            out_ref[0, j] = y[:8] + nacc[0, j]
+            out_ref[1, j] = y[8:] + nacc[1, j]
 
     for cp in m_copy:
         cp.wait_send()
@@ -346,11 +368,17 @@
     rows = leaves * s
     any_spec = pl.BlockSpec(memory_space=pltpu.HBM)
     dma = pltpu.SemaphoreType.DMA
-    return pl.pallas_call(
+    vmem = pl.BlockSpec(memory_space=pltpu.VMEM)
+    parts = pl.pallas_call(
         kernel,
-        out_shape=pltpu.VMEM(sources.shape, F32),
+        out_shape=(
+            pltpu.VMEM(sources.shape, F32),
+            pltpu.VMEM((CHUNK_LEAVES[-1] * s, 2 * rank), F32),
+            pltpu.VMEM((leaves, 4 * rank, size), BF16),
+            pltpu.VMEM(sources.shape, F32),
+        ),
         in_specs=[any_spec] * 8,
-        out_specs=pl.BlockSpec(memory_space=pltpu.VMEM),
+        out_specs=(vmem,) * 4,
         scratch_shapes=[
             pltpu.VMEM(sources.shape, F32),
             pltpu.VMEM((leaves, 2 * rank, size), F32),
@@ -365,8 +393,6 @@
             pltpu.VMEM((2 * HALO, 2, s, size), F32),
             pltpu.VMEM((N_W, 2 * rank, 4 * rank), BF16),
             pltpu.VMEM((2, 2 * rank, 4 * rank), BF16),
-            pltpu.VMEM((leaves, 4 * rank, size), BF16),
-            pltpu.VMEM(sources.shape, F32),
             pltpu.VMEM((Z1 + 1, rows, 2 * rank), F32),
             pltpu.VMEM((N_RECV, rows, 2 * rank), F32),
             pltpu.VMEM((3, rows, 2 * rank), F32),
@@ -387,11 +413,19 @@
             pltpu.SemaphoreType.REGULAR((4,)),
         ],
         compiler_params=pltpu.CompilerParams(
-            collective_id=0, has_side_effects=True, vmem_limit_bytes=60 * 1024 * 1024),
+            collective_id=0, has_side_effects=True, vmem_limit_bytes=54 * 1024 * 1024),
         name="butterfly",
     )(sources, leaf_slot, in_basis.reshape(leaves, 2 * rank, size),
       butterfly.reshape(2 * levels, rank, 2 * rank), out_basis.reshape(leaves, 2 * rank, size),
       near_pairs.T, near_count, near_blocks)
+    return pl.pallas_call(
+        store,
+        out_shape=jax.ShapeDtypeStruct(sources.shape, F32),
+        in_specs=[vmem] * 4,
+        out_specs=any_spec,
+        scratch_shapes=[pltpu.VMEM((2, CHUNK_LEAVES[-1], s, size), F32), dma((4,))],
+        name="store",
+    )(*[pltpu.with_memory_space_constraint(x, pltpu.VMEM) for x in parts])
 
 
 def solution(mesh):

time: 30.1 us -> 30.1 us (level)
  local copies, waits for them, and re-layouts: 0.71 us -> 0 us
  Pallas kernels: 28.6 us -> 29.3 us
    unnamed x1 -> x0, local copies, waits for them, and re-layouts: 0.71 us -> none
    pallas_call x1 -> x2, Pallas kernels: 28.6 us -> 29.3 us  [the longest x1 28.4 us: body(): pl.pallas_call(kernel, out_shape=(pltpu.VMEM(sources.shape, F32), pltpu.V...]
where the time goes in v5:
time: 30.1 us; the launch traced here: 29.9 us
  Pallas kernels  29.3 us (97%)
  between operations  0.66 us (2%)
    pallas_call x1, Pallas kernels, body(): pl.pallas_call(kernel, out_shape=(pltpu.VMEM(sources.shape, F32), pltpu.V...  28.4 us
    pallas_call x1, Pallas kernels, body(): pl.pallas_call(store, out_shape=jax.ShapeDtypeStruct(sources.shape, F32),...  0.9 us

profile of v5, /device:TPU:8, one launch (start us, length us, event | category | flops | bytes accessed | tf_op | source)
XLA Modules:
  0.0 29.9 jit_solution(1902109188094555027)
XLA Ops:
  0.7 28.4 %butterfly.1 = (f32[2,16,8,256]{3,2,1,0:T(8,128)S(1)}, f32[32,128]{1,0:T(8,128)S(1)}, bf16[16,256,256]{2,1,0:T(8,128)(2,1)S(1)}, f32[2,16,8,256]{3,2,1,0:T(8,128)S(1)}) custom-call(f32[2,16,8,256]{3,2,1,0:T(8,128)} %src_hbm.1, s32[4096]{0:T(1024)} %slot_hbm.1, f32[16,128,256]{2,1,0:T(8,128)} %bitcast.4, f32[16,64,128]{2,1,0:T(8,128)} %bitcast.6, ...), custom_call_target="tpu_custom_call" | custom-call | tf_op jit(solution)/shard_map/butterfly/pallas_call | solution.py:372
  29.0 0.9 %store.1 = f32[2,16,8,256]{3,2,1,0:T(8,128)} custom-call(f32[2,16,8,256]{3,2,1,0:T(8,128)S(1)} %get-tuple-element.9.field, f32[32,128]{1,0:T(8,128)S(1)} %get-tuple-element.10.last, bf16[16,256,256]{2,1,0:T(8,128)(2,1)S(1)} %get-tuple-element.11.obf, f32[2,16,8,256]{3,2,1,0:T(8,128)S(1)} %get-tuple-element.12.nacc), custom_call_target="tpu_custom_call" | custom-call | tf_op jit(solution)/shard_map/store/pallas_call | solution.py:421

commit v6 on v5

--- a/solution.py
+++ b/solution.py
@@ -317,6 +317,7 @@
             if i + 1 == Z1 and c >= DIRECT:
                 for k in (1, 0):
                     z_panel[k, chunk(c)] = times([acc], w[W_FAR + k])
+                for k in (1, 0):
                     copy_to(z_panel.at[k], Z2, k, c).start()
 
     background(Z1)

time: 30.1 us -> 30.1 us (level)
  no operation moved by 1% of the time
where the time goes in v6:
time: 30.1 us; the launch traced here: 29.9 us
  Pallas kernels  29.2 us (97%)
  between operations  0.66 us (2%)
    pallas_call x1, Pallas kernels, body(): pl.pallas_call(kernel, out_shape=(pltpu.VMEM(sources.shape, F32), pltpu.V...  28.4 us
    pallas_call x1, Pallas kernels, body(): pl.pallas_call(store, out_shape=jax.ShapeDtypeStruct(sources.shape, F32),...  0.9 us

profile of v6, /device:TPU:8, one launch (start us, length us, event | category | flops | bytes accessed | tf_op | source)
XLA Modules:
  0.0 29.9 jit_solution(955550223726121350)
XLA Ops:
  0.7 28.4 %butterfly.1 = (f32[2,16,8,256]{3,2,1,0:T(8,128)S(1)}, f32[32,128]{1,0:T(8,128)S(1)}, bf16[16,256,256]{2,1,0:T(8,128)(2,1)S(1)}, f32[2,16,8,256]{3,2,1,0:T(8,128)S(1)}) custom-call(f32[2,16,8,256]{3,2,1,0:T(8,128)} %src_hbm.1, s32[4096]{0:T(1024)} %slot_hbm.1, f32[16,128,256]{2,1,0:T(8,128)} %bitcast.4, f32[16,64,128]{2,1,0:T(8,128)} %bitcast.6, ...), custom_call_target="tpu_custom_call" | custom-call | tf_op jit(solution)/shard_map/butterfly/pallas_call | solution.py:373
  29.0 0.9 %store.1 = f32[2,16,8,256]{3,2,1,0:T(8,128)} custom-call(f32[2,16,8,256]{3,2,1,0:T(8,128)S(1)} %get-tuple-element.9.field, f32[32,128]{1,0:T(8,128)S(1)} %get-tuple-element.10.last, bf16[16,256,256]{2,1,0:T(8,128)(2,1)S(1)} %get-tuple-element.11.obf, f32[2,16,8,256]{3,2,1,0:T(8,128)S(1)} %get-tuple-element.12.nacc), custom_call_target="tpu_custom_call" | custom-call | tf_op jit(solution)/shard_map/store/pallas_call | solution.py:422
